TPU v7x, 512 devices: a whole 4x4x16 slice. The times are simulated.
512 devices in a mesh: grp: 8 (over x, core), dom: 64 (over y, z).
Axes of the slice: x: 4, y: 4, z: 16, core: 2. Of those that a mesh axis runs over, the one named last changes fastest.
Arguments:
- nodes: bfloat16 [131072, 512], P(('grp', 'dom')), may hold values from -6 to 6
- w_send: bfloat16 [512, 256], replicated, may hold values from -0.1875 to 0.1875
- w_recv: bfloat16 [512, 256], replicated, may hold values from -0.1875 to 0.1875
- edge_bias: float32 [256], replicated, may hold values from -4 to 4
- w_msg: bfloat16 [256, 512], replicated, may hold values from -0.375 to 0.375
- msg_gain: float32 [512], replicated, may hold values from 0.5 to 1.5
- w_self: bfloat16 [512, 512], replicated, may hold values from -0.1875 to 0.1875
- w_agg: bfloat16 [512, 512], replicated, may hold values from -0.09375 to 0.09375
- w_coarse_in: bfloat16 [512, 256], replicated, may hold values from -0.25 to 0.25
- coarse_bias: float32 [256], replicated, may hold values from -4 to 4
- w_coarse_out: bfloat16 [256, 512], replicated, may hold values from -0.375 to 0.375
- halo_send: int32 [512, 2, 128], P(('grp', 'dom')), may hold values from 0 to 255
- neighbours: int32 [131072, 8], P(('grp', 'dom')), may hold values from 0 to 511
- edge_mask: int32 [131072, 8], P(('grp', 'dom')), may hold values 0 or 1
- restrict_ids: int32 [131072], P(('grp', 'dom')), may hold values from 0 to 31
- coarse_holder_index: int32 [32768, 1], P(('grp', 'dom')), may hold values from 0 to 63; in each aligned block of 64 rows (0 to 63, 64 to 127, ...) at most 2 rows name the same one
- coarse_slot: int32 [32768, 1], P(('grp', 'dom')), may hold values from 0 to 15
Outputs:
- updated: bfloat16 [131072, 512], P(('grp', 'dom'))
Inputs may be any that keep to these rules, and one draw needn't show every extreme that they name: `coarse_holder_index`: among the restricted rows of one partition no owner is named more than 2 times, and in every draw some owner is named exactly 2 times.
All inputs are finite; a program needn't handle non-finite values. No bound on the sum of `edge_mask` on one device may be relied on, other than what follows from the above.
Results may differ from a plain program's by a relative error of at most 0.0053.
Values may be sent and summed in bfloat16 or wider, within the bound.
A program may use at most 64 MiB of HBM per device.

v0:
```python
import jax
import jax.numpy as jnp
from jax import lax
from jax.sharding import PartitionSpec as P

RBLOCK = 128
RCOARSE = 32


def padded(x, sides, width):
    for axis, dim in sides:
        size, length = (lax.axis_size(axis), x.shape[dim])
        up = [(i, (i + 1) % size) for i in range(size)]
        down = [(j, i) for i, j in up]
        last = lax.slice_in_dim(x, length - width, length, axis=dim)
        initial = lax.slice_in_dim(x, 0, width, axis=dim)
        before = lax.ppermute(last, axis, up)
        after = lax.ppermute(initial, axis, down)
        x = jnp.concatenate([before, x, after], axis=dim)
    return x


def local(
    nodes,
    w_send,
    w_recv,
    edge_bias,
    w_msg,
    msg_gain,
    w_self,
    w_agg,
    w_coarse_in,
    coarse_bias,
    w_coarse_out,
    halo_send,
    neighbours,
    edge_mask,
    restrict_ids,
    coarse_holder_index,
    coarse_slot,
):
    count = nodes.shape[0]
    width = nodes.shape[1]
    proj = jnp.dot(nodes, w_send, preferred_element_type=jnp.float32).astype(jnp.bfloat16)
    recv_part = jnp.dot(nodes, w_recv, preferred_element_type=jnp.float32)
    picks = halo_send[0]
    extended = padded(nodes[picks], (("grp", 0),), 1)
    from_lower = jnp.dot(extended[0], w_send, preferred_element_type=jnp.float32).astype(
        jnp.bfloat16
    )
    upper_level_input = jnp.dot(extended[3], w_send, preferred_element_type=jnp.float32).astype(
        jnp.bfloat16
    )
    table = jnp.concatenate([proj, from_lower, upper_level_input], axis=0)
    agg = jnp.zeros((count, width), jnp.float32)
    for slot in range(neighbours.shape[1]):
        pre = table[neighbours[:, slot]].astype(jnp.float32) + recv_part + edge_bias
        hidden = jax.nn.silu(pre).astype(jnp.bfloat16)
        message = jnp.dot(hidden, w_msg, preferred_element_type=jnp.float32)
        mean = jnp.mean(message, axis=1, keepdims=True)
        var = jnp.mean((message - mean) ** 2, axis=1, keepdims=True)
        normed = (message - mean) / jnp.sqrt(var + 1e-05) * msg_gain
        agg = agg + normed * edge_mask[:, slot : slot + 1].astype(jnp.float32)
    agg = agg.astype(jnp.bfloat16)
    change = jax.nn.silu(
        jnp.dot(nodes, w_self, preferred_element_type=jnp.float32)
        + jnp.dot(agg, w_agg, preferred_element_type=jnp.float32)
    )
    blocks = count // RBLOCK
    member = (
        restrict_ids.reshape(blocks, RBLOCK)[:, :, None]
        == jnp.arange(RCOARSE, dtype=jnp.int32)[None, None, :]
    ).astype(jnp.bfloat16)
    restricted = jnp.einsum(
        "bic,bid->bcd",
        member,
        nodes.reshape(blocks, RBLOCK, width),
        preferred_element_type=jnp.float32,
    )
    restricted = (restricted * 0.25).astype(jnp.bfloat16).reshape(blocks * RCOARSE, width)
    node_rows = restricted.shape[0]
    group_partners = lax.axis_size("dom")
    slot_limit = max(2, 2 * node_rows // group_partners)
    slot_count = node_rows // 4
    owner = coarse_holder_index[:, 0]
    target = coarse_slot[:, 0]
    order = jnp.arange(node_rows, dtype=jnp.int32)
    earlier = (owner[None, :] == owner[:, None]) & (order[None, :] < order[:, None])
    rank = jnp.sum(earlier.astype(jnp.int32), axis=1)
    slot_index = owner * slot_limit + rank
    placed = (
        jnp.arange(group_partners * slot_limit, dtype=jnp.int32)[:, None] == slot_index[None, :]
    )
    place_mat = placed.astype(jnp.bfloat16)
    slot_buf = jnp.sum(jnp.where(placed, target[None, :] + 1, 0), axis=1) - 1
    slot_buf = slot_buf.reshape(group_partners, slot_limit)
    outgoing = jnp.dot(place_mat, restricted, preferred_element_type=jnp.float32).astype(
        jnp.bfloat16
    )
    got_rows, received_slot = (
        lax.all_to_all(
            outgoing.reshape(group_partners, slot_limit, width),
            "dom",
            split_axis=0,
            concat_axis=0,
            tiled=True,
        ),
        lax.all_to_all(slot_buf, "dom", split_axis=0, concat_axis=0, tiled=True),
    )
    got_proj = jnp.dot(
        got_rows.reshape(group_partners * slot_limit, width),
        w_coarse_in,
        preferred_element_type=jnp.float32,
    ).astype(jnp.bfloat16)
    member_coarse = (
        received_slot.reshape(1, group_partners * slot_limit)
        == jnp.arange(slot_count, dtype=jnp.int32)[:, None]
    ).astype(jnp.bfloat16)
    summed = jnp.dot(member_coarse, got_proj, preferred_element_type=jnp.float32)
    coarse_hid = jax.nn.silu(summed + coarse_bias).astype(jnp.bfloat16)
    coarse_out = jnp.dot(coarse_hid, w_coarse_out, preferred_element_type=jnp.float32).astype(
        jnp.bfloat16
    )
    back = jnp.dot(member_coarse.T, coarse_out, preferred_element_type=jnp.float32).astype(
        jnp.bfloat16
    )
    returned = lax.all_to_all(
        back.reshape(group_partners, slot_limit, width),
        "dom",
        split_axis=0,
        concat_axis=0,
        tiled=True,
    )
    returned_rows = returned.reshape(group_partners * slot_limit, width)
    corr_rows = jnp.dot(place_mat.T, returned_rows, preferred_element_type=jnp.float32).astype(
        jnp.bfloat16
    )
    corr_nodes = jnp.einsum(
        "bic,bcd->bid",
        member,
        corr_rows.reshape(blocks, RCOARSE, width),
        preferred_element_type=jnp.float32,
    ).reshape(count, width)
    return (nodes.astype(jnp.float32) + change + corr_nodes).astype(jnp.bfloat16)


def solution(mesh):
    return jax.shard_map(
        local,
        mesh=mesh,
        in_specs=(
            P(("grp", "dom"), None),
            P(),
            P(),
            P(),
            P(),
            P(),
            P(),
            P(),
            P(),
            P(),
            P(),
            P(("grp", "dom"), None, None),
            P(("grp", "dom"), None),
            P(("grp", "dom"), None),
            P(("grp", "dom")),
            P(("grp", "dom"), None),
            P(("grp", "dom"), None),
        ),
        out_specs=P(("grp", "dom"), None),
        check_vma=False,
    )
```

profile of v0, /device:TPU:6, one launch (start us, length us, event | category | flops | bytes accessed | tf_op | source)
XLA Modules:
  0.0 113.4 jit_solution(8942758266007237902)
XLA Ops:
  0.0 0.7 add_bitcast_fusion
  1.7 0.7 sub.53
  2.4 18.9 %all-to-all-start = ((s32[64,1,2]{2,1,0:T(1,128)}), s32[64,1,2]{2,1,0:T(1,128)S(1)}, u32[]{:S(2)}, u32[]{:S(2)}) async-start(s32[64,1,2]{2,1,0:T(1,128)} %bitcast.25), calls=%async_computation | async-start | bytes 65536 | tf_op jit(solution)/shard_map/all_to_all | solution.py:108
  21.3 2.2 %gather_fusion = bf16[256,512]{1,0:T(8,128)(2,1)S(1)} fusion(bf16[256,512]{1,0:T(8,128)(2,1)} %param.17, s32[1024]{0:T(1024)S(1)} %pad_clamp_fusion.8), kind=kCustom, calls=%fused_computation | custom fusion | bytes 525312 | tf_op jit(solution)/shard_map/gather | solution.py:47
  23.6 1.7 %collective-permute-start.1 = (bf16[1,128,512]{2,1,0:T(8,128)(2,1)S(1)}, bf16[1,128,512]{2,1,0:T(8,128)(2,1)S(1)}, u32[]{:S(2)}, u32[]{:S(2)}) collective-permute-start(bf16[1,128,512]{2,1,0:T(8,128)(2,1)S(1)} %get-tuple-element.6), channel_id=1, source_target_pairs={{64,0},{128,64},{192,128},{256,192},{320,256},{384,320},{448,384},... | collective-permute-start | bytes 393224 | tf_op jit(solution)/shard_map/ppermute | solution.py:18
  28.6 0.7 copy-done.7
  30.6 5.1 %all-to-all-done = s32[64,1,2]{2,1,0:T(1,128)S(1)} async-done(((s32[64,1,2]{2,1,0:T(1,128)}), s32[64,1,2]{2,1,0:T(1,128)S(1)}, u32[]{:S(2)}, u32[]{:S(2)}) %all-to-all-start) | async-done | bytes 544 | tf_op jit(solution)/shard_map/all_to_all | solution.py:108
  35.7 10.2 %all-to-all-start.1 = ((bf16[64,2,512]{2,1,0:T(2,128)(2,1)}), bf16[64,2,512]{2,1,0:T(2,128)(2,1)S(1)}, u32[]{:S(2)}, u32[]{:S(2)}) async-start(bf16[64,2,512]{2,1,0:T(2,128)(2,1)} %reshape.191), calls=%async_computation.1 | async-start | bytes 262144 | tf_op jit(solution)/shard_map/all_to_all | solution.py:101
  46.5 0.8 reduce.3
  47.9 1.2 %gather_fusion.8 = bf16[256,256]{1,0:T(8,128)(2,1)S(1)} fusion(bf16[512,256]{1,0:T(8,128)(2,1)S(1)} %pad_maximum_fusion, s32[1024]{0:T(1024)S(1)} %pad_clamp_fusion), kind=kCustom, calls=%fused_computation.8 | custom fusion | bytes 263168 | tf_op jit(solution)/shard_map/gather | solution.py:57
  49.0 1.2 %gather_fusion.7 = bf16[256,256]{1,0:T(8,128)(2,1)S(1)} fusion(bf16[512,256]{1,0:T(8,128)(2,1)S(1)} %pad_maximum_fusion, s32[1024]{0:T(1024)S(1)} %pad_clamp_fusion.1), kind=kCustom, calls=%fused_computation.7 | custom fusion | bytes 263168 | tf_op jit(solution)/shard_map/gather | solution.py:57
  50.2 1.2 %gather_fusion.6 = bf16[256,256]{1,0:T(8,128)(2,1)S(1)} fusion(bf16[512,256]{1,0:T(8,128)(2,1)S(1)} %pad_maximum_fusion, s32[1024]{0:T(1024)S(1)} %pad_clamp_fusion.2), kind=kCustom, calls=%fused_computation.6 | custom fusion | bytes 263168 | tf_op jit(solution)/shard_map/gather | solution.py:57
  51.3 1.8 %gather_fusion.5 = bf16[256,256]{1,0:T(8,128)(2,1)} fusion(bf16[512,256]{1,0:T(8,128)(2,1)S(1)} %pad_maximum_fusion, s32[1024]{0:T(1024)S(1)} %pad_clamp_fusion.3), kind=kCustom, calls=%fused_computation.5 | custom fusion | bytes 263168 | tf_op jit(solution)/shard_map/gather | solution.py:57
  53.1 1.8 %gather_fusion.4 = bf16[256,256]{1,0:T(8,128)(2,1)} fusion(bf16[512,256]{1,0:T(8,128)(2,1)S(1)} %pad_maximum_fusion, s32[1024]{0:T(1024)S(1)} %pad_clamp_fusion.4), kind=kCustom, calls=%fused_computation.4 | custom fusion | bytes 263168 | tf_op jit(solution)/shard_map/gather | solution.py:57
  54.9 1.8 %gather_fusion.3 = bf16[256,256]{1,0:T(8,128)(2,1)} fusion(bf16[512,256]{1,0:T(8,128)(2,1)S(1)} %pad_maximum_fusion, s32[1024]{0:T(1024)S(1)} %pad_clamp_fusion.5), kind=kCustom, calls=%fused_computation.3 | custom fusion | bytes 263168 | tf_op jit(solution)/shard_map/gather | solution.py:57
  56.7 1.8 %gather_fusion.2 = bf16[256,256]{1,0:T(8,128)(2,1)} fusion(bf16[512,256]{1,0:T(8,128)(2,1)S(1)} %pad_maximum_fusion, s32[1024]{0:T(1024)S(1)} %pad_clamp_fusion.6), kind=kCustom, calls=%fused_computation.2 | custom fusion | bytes 263168 | tf_op jit(solution)/shard_map/gather | solution.py:57
  58.5 1.8 %gather_fusion.1 = bf16[256,256]{1,0:T(8,128)(2,1)} fusion(bf16[512,256]{1,0:T(8,128)(2,1)S(1)} %pad_maximum_fusion, s32[1024]{0:T(1024)S(1)} %pad_clamp_fusion.7), kind=kCustom, calls=%fused_computation.1 | custom fusion | bytes 263168 | tf_op jit(solution)/shard_map/gather | solution.py:57
  62.7 1.4 %fusion.50 = (f32[256]{0:T(256)S(1)}, f32[256,512]{1,0:T(8,128)S(1)}) fusion(bf16[256,512]{1,0:T(8,128)(2,1)S(1)} %copy-done.56, f32[256,256]{1,0:T(8,128)} %copy-done.8, bf16[256,256]{1,0:T(8,128)(2,1)S(1)} %copy-done.14, f32[256]{0:T(256)S(1)} %copy-done.59), kind=kOutput, calls=%fused_computation.142 | convolution fusion | flops 67763968 | bytes 1181696 | tf_op jit(solution)/shard_map/dot_general | solution.py:59
  66.8 1.1 fusion.54
  69.3 0.8 multiply_reduce_fusion.4
  70.0 0.7 multiply_reduce_fusion.5
  70.8 0.7 multiply_reduce_fusion.6
  72.7 0.7 reshape.192
  73.4 1.3 %multiply_convert_fusion.16 = bf16[16,256]{1,0:T(8,128)(2,1)S(1)} fusion(bf16[128,512]{1,0:T(8,128)(2,1)} %reshape.192, bf16[512,256]{1,0:T(8,128)(2,1)} %param.25, f32[256]{0:T(256)} %param.26, s32[128]{0:T(128)S(1)} %eq.66), kind=kOutput, calls=%fused_computation.77 | convolution fusion | flops 34662400 | bytes 402944 | tf_op jit(solution)/shard_map/dot_general | solution.py:119
  74.7 1.3 %convolution_convert_fusion = bf16[128,512]{1,0:T(8,128)(2,1)S(1)} fusion(bf16[16,256]{1,0:T(8,128)(2,1)S(1)} %multiply_convert_fusion.16, bf16[256,512]{1,0:T(8,128)(2,1)} %param.27, s32[128]{0:T(128)S(1)} %eq.66), kind=kOutput, calls=%fused_computation.10 | convolution fusion | flops 6367232 | bytes 401920 | tf_op jit(solution)/shard_map/dot_general | solution.py:124
  75.9 0.7 reshape.193
  76.6 15.0 %all-to-all-start.2 = ((bf16[64,2,512]{2,1,0:T(2,128)(2,1)}), bf16[64,2,512]{2,1,0:T(2,128)(2,1)S(1)}, u32[]{:S(2)}, u32[]{:S(2)}) async-start(bf16[64,2,512]{2,1,0:T(2,128)(2,1)} %reshape.193), calls=%async_computation.2 | async-start | bytes 262144 | tf_op jit(solution)/shard_map/all_to_all | solution.py:127
  92.3 1.2 %multiply_reduce_fusion.7 = f32[256]{0:T(256)S(1)} fusion(f32[256,512]{1,0:T(8,128)} %get-tuple-element.38, f32[256]{0:T(256)S(1)} %copy-done.32), kind=kLoop, calls=%fused_computation.32 | loop fusion | flops 392960 | bytes 526336 | tf_op jit(solution)/shard_map/reduce_sum | solution.py:61
  94.8 12.1 %all-to-all-done.2 = bf16[64,2,512]{2,1,0:T(2,128)(2,1)S(1)} async-done(((bf16[64,2,512]{2,1,0:T(2,128)(2,1)}), bf16[64,2,512]{2,1,0:T(2,128)(2,1)S(1)}, u32[]{:S(2)}, u32[]{:S(2)}) %all-to-all-start.2) | async-done | bytes 131104 | tf_op jit(solution)/shard_map/all_to_all | solution.py:127
  106.8 0.7 reshape.194
  107.5 1.2 %convolution_convert_fusion.6 = bf16[64,512]{1,0:T(8,128)(2,1)S(1)} fusion(bf16[128,512]{1,0:T(8,128)(2,1)} %reshape.194, s32[64]{0:T(128)S(1)} %copy-done.37), kind=kOutput, calls=%fused_computation.18 | convolution fusion | flops 8429568 | bytes 196864 | tf_op jit(solution)/shard_map/dot_general | solution.py:135
  109.9 3.5 %fusion.3 = bf16[256,512]{1,0:T(8,128)(2,1)} fusion(f32[2,128,512]{2,1,0:T(8,128)S(1)} %fusion.30, f32[256,512]{1,0:T(8,128)S(1)} %fusion.55, bf16[512,512]{1,0:T(8,128)(2,1)} %param.24, bf16[256,512]{1,0:T(8,128)(2,1)S(1)} %copy-done.1, f32[256,512]{1,0:T(8,128)S(1)} %get-tuple-element.24, f32[256,512]{1,0:T(8,128)S(1)} %get-tuple-element.26, ...), kind=kOutput, calls=%fused_computation.23 | convolution fusion | flops 140640256 | bytes 6318080 | tf_op jit(solution)/shard_map/dot_general | solution.py:67
  (176 shorter events, 16.9 us)
Async XLA Ops:
  0.0 29.6 %copy-start = (bf16[512,512]{1,0:T(8,128)(2,1)S(1)}, bf16[512,512]{1,0:T(8,128)(2,1)}, u32[]{:S(2)}) copy-start(bf16[512,512]{1,0:T(8,128)(2,1)} %param.23) | copy-start | bytes 1572868
  1.6 26.0 %copy-start.36 = (s32[64]{0:T(128)}, s32[64]{0:T(128)S(1)}, u32[]{:S(2)}) copy-start(s32[64]{0:T(128)S(1)} %multiply_add_fusion) | copy-start | bytes 772
  2.4 18.9 %copy-start.46 = (s32[1,2,128]{2,1,0:T(2,128)S(1)}, s32[1,2,128]{2,1,0:T(2,128)}, u32[]{:S(2)}) copy-start(s32[1,2,128]{2,1,0:T(2,128)} %param.28) | copy-start | bytes 3076
  2.4 33.3 %all-to-all-start = ((s32[64,1,2]{2,1,0:T(1,128)}), s32[64,1,2]{2,1,0:T(1,128)S(1)}, u32[]{:S(2)}, u32[]{:S(2)}) async-start(s32[64,1,2]{2,1,0:T(1,128)} %bitcast.25), calls=%async_computation | async-start | bytes 65536 | tf_op jit(solution)/shard_map/all_to_all | solution.py:108
  23.5 1.8 %copy-start.15 = (s32[256,8]{0,1:T(8,128)S(1)}, s32[256,8]{0,1:T(8,128)}, u32[]{:S(2)}) copy-start(s32[256,8]{0,1:T(8,128)} %param.29) | copy-start | bytes 24580
  23.5 3.2 %copy-start.1 = (bf16[256,512]{1,0:T(8,128)(2,1)S(1)}, bf16[256,512]{1,0:T(8,128)(2,1)}, u32[]{:S(2)}) copy-start(bf16[256,512]{1,0:T(8,128)(2,1)} %param.17) | copy-start | bytes 786436
  23.6 23.9 %collective-permute-start = (bf16[1,128,512]{2,1,0:T(8,128)(2,1)S(1)}, bf16[1,128,512]{2,1,0:T(8,128)(2,1)S(1)}, u32[]{:S(2)}, u32[]{:S(2)}) collective-permute-start(bf16[1,128,512]{2,1,0:T(8,128)(2,1)S(1)} %get-tuple-element.5), channel_id=1, source_target_pairs={{0,64},{64,128},{128,192},{192,256},{256,320},{320,384},{384,448},... | collective-permute-start | bytes 393224 | tf_op jit(solution)/shard_map/ppermute | solution.py:17
  23.6 24.0 %collective-permute-start.1 = (bf16[1,128,512]{2,1,0:T(8,128)(2,1)S(1)}, bf16[1,128,512]{2,1,0:T(8,128)(2,1)S(1)}, u32[]{:S(2)}, u32[]{:S(2)}) collective-permute-start(bf16[1,128,512]{2,1,0:T(8,128)(2,1)S(1)} %get-tuple-element.6), channel_id=1, source_target_pairs={{64,0},{128,64},{192,128},{256,192},{320,256},{384,320},{448,384},... | collective-permute-start | bytes 393224 | tf_op jit(solution)/shard_map/ppermute | solution.py:18
  27.4 0.9 copy-start.2
  28.4 0.9 copy-start.7
  29.6 31.5 %copy-start.8 = (f32[256,256]{1,0:T(8,128)}, f32[256,256]{1,0:T(8,128)S(1)}, u32[]{:S(2)}) copy-start(f32[256,256]{1,0:T(8,128)S(1)} %fusion.56) | copy-start | bytes 786436
  35.7 36.9 %all-to-all-start.1 = ((bf16[64,2,512]{2,1,0:T(2,128)(2,1)}), bf16[64,2,512]{2,1,0:T(2,128)(2,1)S(1)}, u32[]{:S(2)}, u32[]{:S(2)}) async-start(bf16[64,2,512]{2,1,0:T(2,128)(2,1)} %reshape.191), calls=%async_computation.1 | async-start | bytes 262144 | tf_op jit(solution)/shard_map/all_to_all | solution.py:101
  58.5 1.8 %copy-start.55 = (bf16[256,512]{1,0:T(8,128)(2,1)S(1)}, bf16[256,512]{1,0:T(8,128)(2,1)}, u32[]{:S(2)}) copy-start(bf16[256,512]{1,0:T(8,128)(2,1)} %param.21) | copy-start | bytes 786436
  58.5 1.8 %copy-start.58 = (f32[256]{0:T(256)S(1)}, f32[256]{0:T(256)}, u32[]{:S(2)}) copy-start(f32[256]{0:T(256)} %param.20) | copy-start | bytes 3076
  60.7 7.7 %copy-start.18 = (f32[256]{0:T(256)}, f32[256]{0:T(256)S(1)}, u32[]{:S(2)}) copy-start(f32[256]{0:T(256)S(1)} %broadcast_multiply_fusion) | copy-start | bytes 3076
  60.7 1.0 copy-start.56
  61.7 6.9 %copy-start.20 = (f32[256]{0:T(256)}, f32[256]{0:T(256)S(1)}, u32[]{:S(2)}) copy-start(f32[256]{0:T(256)S(1)} %broadcast_multiply_fusion.1) | copy-start | bytes 3076
  62.7 6.2 %copy-start.22 = (f32[256]{0:T(256)}, f32[256]{0:T(256)S(1)}, u32[]{:S(2)}) copy-start(f32[256]{0:T(256)S(1)} %broadcast_multiply_fusion.2) | copy-start | bytes 3076
  62.7 1.4 %copy-start.9 = (f32[256,256]{1,0:T(8,128)S(1)}, f32[256,256]{1,0:T(8,128)}, u32[]{:S(2)}) copy-start(f32[256,256]{1,0:T(8,128)} %copy-done.8) | copy-start | bytes 786436
  62.7 1.4 %copy-start.13 = (bf16[256,256]{1,0:T(8,128)(2,1)S(1)}, bf16[256,256]{1,0:T(8,128)(2,1)}, u32[]{:S(2)}) copy-start(bf16[256,256]{1,0:T(8,128)(2,1)} %gather_fusion.4) | copy-start | bytes 393220
  64.0 5.0 %copy-start.24 = (f32[256]{0:T(256)}, f32[256]{0:T(256)S(1)}, u32[]{:S(2)}) copy-start(f32[256]{0:T(256)S(1)} %broadcast_multiply_fusion.3) | copy-start | bytes 3076
  64.4 4.9 %copy-start.3 = (f32[256,512]{1,0:T(8,128)}, f32[256,512]{1,0:T(8,128)S(1)}, u32[]{:S(2)}) copy-start(f32[256,512]{1,0:T(8,128)S(1)} %get-tuple-element.32) | copy-start | bytes 1572868
  65.0 4.3 %copy-start.26 = (f32[256]{0:T(256)}, f32[256]{0:T(256)S(1)}, u32[]{:S(2)}) copy-start(f32[256]{0:T(256)S(1)} %broadcast_multiply_fusion.4) | copy-start | bytes 3076
  65.3 4.7 %copy-start.5 = (f32[256,512]{1,0:T(8,128)}, f32[256,512]{1,0:T(8,128)S(1)}, u32[]{:S(2)}) copy-start(f32[256,512]{1,0:T(8,128)S(1)} %get-tuple-element.34) | copy-start | bytes 1572868
  65.9 4.2 %copy-start.28 = (f32[256]{0:T(256)}, f32[256]{0:T(256)S(1)}, u32[]{:S(2)}) copy-start(f32[256]{0:T(256)S(1)} %broadcast_multiply_fusion.5) | copy-start | bytes 3076
  66.2 4.6 %copy-start.6 = (f32[256,512]{1,0:T(8,128)}, f32[256,512]{1,0:T(8,128)S(1)}, u32[]{:S(2)}) copy-start(f32[256,512]{1,0:T(8,128)S(1)} %get-tuple-element.36) | copy-start | bytes 1572868
  66.8 4.0 %copy-start.30 = (f32[256]{0:T(256)}, f32[256]{0:T(256)S(1)}, u32[]{:S(2)}) copy-start(f32[256]{0:T(256)S(1)} %broadcast_multiply_fusion.6) | copy-start | bytes 3076
  76.6 30.2 %all-to-all-start.2 = ((bf16[64,2,512]{2,1,0:T(2,128)(2,1)}), bf16[64,2,512]{2,1,0:T(2,128)(2,1)S(1)}, u32[]{:S(2)}, u32[]{:S(2)}) async-start(bf16[64,2,512]{2,1,0:T(2,128)(2,1)} %reshape.193), calls=%async_computation.2 | async-start | bytes 262144 | tf_op jit(solution)/shard_map/all_to_all | solution.py:127
  92.3 1.2 %copy-start.34 = (f32[256]{0:T(256)S(1)}, f32[256]{0:T(256)}, u32[]{:S(2)}) copy-start(f32[256]{0:T(256)} %multiply_reduce_fusion.4) | copy-start | bytes 3076
  92.3 1.3 %copy-start.35 = (f32[256]{0:T(256)S(1)}, f32[256]{0:T(256)}, u32[]{:S(2)}) copy-start(f32[256]{0:T(256)} %multiply_reduce_fusion.5) | copy-start | bytes 3076
  94.8 12.8 %copy-start.37 = (s32[64]{0:T(128)S(1)}, s32[64]{0:T(128)}, u32[]{:S(2)}) copy-start(s32[64]{0:T(128)} %copy-done.36) | copy-start | bytes 772
  107.5 1.7 %copy-start.4 = (f32[256,512]{1,0:T(8,128)S(1)}, f32[256,512]{1,0:T(8,128)}, u32[]{:S(2)}) copy-start(f32[256,512]{1,0:T(8,128)} %copy-done.3) | copy-start | bytes 1572868
  (34 other events, 23.6 us)
where the time goes:
time: 115 us; the launch traced here: 113 us
  starting transfers between devices  45.8 us (40%)
  local copies, waits for them, and re-layouts  26.5 us (23%)
  waiting for transfers between devices  17.2 us (15%)
  matrix products  13.4 us (12%)
  other arithmetic  9.69 us (8%)
    all_to_all x1, starting transfers between devices, local(): lax.all_to_all(slot_buf, 'dom', split_axis=0, concat_axis=0, tiled=True)  18.9 us
    all_to_all x1, starting transfers between devices, local(): lax.all_to_all(back.reshape(group_partners, slot_limit, width), 'dom', sp...  15 us
    gather x8, local copies, waits for them, and re-layouts, local(): pre = table[neighbours[:, slot]].astype(jnp.float32) + recv_part + edge_bias  12.5 us
    all_to_all x1, waiting for transfers between devices, local(): lax.all_to_all(back.reshape(group_partners, slot_limit, width), 'dom', sp...  12.1 us
    all_to_all x1, starting transfers between devices, local(): lax.all_to_all(outgoing.reshape(group_partners, slot_limit, width), 'dom'...  10.2 us
    unnamed x122, local copies, waits for them, and re-layouts  7.57 us
    all_to_all x1, waiting for transfers between devices, local(): lax.all_to_all(slot_buf, 'dom', split_axis=0, concat_axis=0, tiled=True)  5.13 us
    dot_general x8, matrix products, local(): message = jnp.dot(hidden, w_msg, preferred_element_type=jnp.float32)  4.39 us
  transfers between devices with their start and end apart: 5, of which 2 were waited for; matrix products, arithmetic and copies ran while one was open for 27% of the time, Pallas kernels for 0%

commit v1 on v0

v1 whole, which is shorter than its diff:
```python
import jax
import jax.numpy as jnp
from jax import lax
from jax.experimental import pallas as pl
from jax.experimental.pallas import tpu as pltpu
from jax.sharding import PartitionSpec as P

MESH = pl.DeviceIdType.MESH
BF = jnp.bfloat16
F32 = jnp.float32
I32 = jnp.int32

GRP = 8
DOM = 64
ZS = 16
YS = 4
N = 256
D = 512
EH = 256
H = 128
DEG = 8
ROWS = 64
RC = 32
RB = 128
SLOTS = 16
MSG = EH + 128


def iota(shape, dim):
    return lax.broadcasted_iota(I32, shape, dim)


def dot(a, b):
    return jnp.dot(a, b, preferred_element_type=F32)


def silu(v):
    return v * (0.5 + 0.5 * jnp.tanh(0.5 * v))


def kernel(
    nodes_h,
    w_send_h,
    w_recv_h,
    w_msg_h,
    w_self_h,
    w_agg_h,
    w_cin_h,
    w_cout_h,
    edge_bias,
    gain,
    coarse_bias,
    halo_ids,
    nbr,
    mask,
    ids,
    own,
    slot,
    out,
    nodes,
    w_send,
    w_recv,
    w_msg,
    w_self,
    w_agg,
    w_cin,
    w_cout,
    table,
    halo_out,
    send_buf,
    recv_buf,
    back_buf,
    ret_buf,
    agg,
    base,
    load_sem,
    halo_ssem,
    halo_rsem,
    c_ssem,
    c_rsem,
    r_ssem,
    r_rsem,
    own_sem,
):
    g = lax.axis_index("grp")
    me = lax.axis_index("dom")
    lower = lax.rem(g + GRP - 1, GRP)
    upper = lax.rem(g + 1, GRP)

    loads = {}
    for i, (name, src, dst) in enumerate(
        (
            ("nodes", nodes_h, nodes),
            ("w_cin", w_cin_h, w_cin),
            ("w_send", w_send_h, w_send),
            ("w_recv", w_recv_h, w_recv),
            ("w_msg", w_msg_h, w_msg),
            ("w_self", w_self_h, w_self),
            ("w_agg", w_agg_h, w_agg),
            ("w_cout", w_cout_h, w_cout),
        )
    ):
        loads[name] = pltpu.make_async_copy(src, dst, load_sem.at[i])
        loads[name].start()

    barrier = pltpu.get_barrier_semaphore()

    def greet(k, carry):
        pl.semaphore_signal(
            barrier, inc=1, device_id=(g, lax.rem(me + k, DOM)), device_id_type=MESH
        )
        return carry

    lax.fori_loop(1, DOM, greet, 0)
    for t in (lower, upper):
        pl.semaphore_signal(barrier, inc=1, device_id=(t, me), device_id_type=MESH)

    own_row = own[...].astype(F32)
    eye = iota((ROWS, ROWS), 0) == iota((ROWS, ROWS), 1)
    own_col = jnp.sum(jnp.where(eye, own_row, 0.0), axis=1, keepdims=True)
    before = (own_col == own_row) & (iota((ROWS, ROWS), 0) < iota((ROWS, ROWS), 1))
    rank = jnp.sum(before.astype(F32), axis=0, keepdims=True)
    pos = (own_row * 2.0 + rank).astype(I32)
    placed = iota((2 * DOM, ROWS), 0) == pos
    place = placed.astype(F32).astype(BF)
    slot_col = (
        jnp.sum(jnp.where(placed, slot[...].astype(F32) + 1.0, 0.0), axis=1, keepdims=True) - 1.0
    )
    row_of = ids[...] + (iota((1, N), 1) // RB) * RC
    member = (iota((ROWS, N), 0) == row_of).astype(F32).astype(BF)
    spread = dot(place, member).T.astype(BF)

    loads["nodes"].wait()
    restricted = (dot(member, nodes[...]) * 0.25).astype(BF)
    loads["w_cin"].wait()
    coarse_in = dot(restricted, w_cin[...]).astype(BF)
    outgoing = dot(place, coarse_in).astype(BF)
    send_buf[:, :, 0:EH] = outgoing.reshape(DOM, 2, EH)
    send_buf[:, :, EH:MSG] = (
        jnp.broadcast_to(slot_col, (2 * DOM, 128)).astype(BF).reshape(DOM, 2, 128)
    )

    loads["w_send"].wait()
    proj = dot(nodes[...], w_send[...]).T.astype(BF)
    table[:, 0:N] = proj
    for i in range(2):
        pick = (iota((N, H), 0) == halo_ids[0, i : i + 1, :]).astype(F32).astype(BF)
        halo_out[i] = dot(proj, pick).astype(BF)

    pl.semaphore_wait(barrier, DOM - 1 + 2)

    mine = pltpu.make_async_copy(send_buf.at[me], recv_buf.at[me], own_sem.at[0])
    mine.start()

    def send_rows(k, carry):
        t = lax.rem(me + k, DOM)
        pltpu.make_async_remote_copy(
            src_ref=send_buf.at[t],
            dst_ref=recv_buf.at[me],
            send_sem=c_ssem,
            recv_sem=c_rsem,
            device_id=(g, t),
            device_id_type=MESH,
        ).start()
        return carry

    lax.fori_loop(1, DOM, send_rows, 0)

    halos = []
    for i, t in ((0, lower), (1, upper)):
        c = pltpu.make_async_remote_copy(
            src_ref=halo_out.at[i],
            dst_ref=table.at[:, pl.ds(N + H * (1 - i), H)],
            send_sem=halo_ssem.at[i],
            recv_sem=halo_rsem.at[i],
            device_id=(t, me),
            device_id_type=MESH,
        )
        c.start()
        halos.append(c)

    loads["w_recv"].wait()
    recv = (dot(nodes[...], w_recv[...]) + edge_bias[...]).T
    loads["w_self"].wait()
    base[...] = dot(nodes[...], w_self[...])
    loads["w_msg"].wait()
    w_msg_t = w_msg[...].T
    agg[...] = jnp.zeros_like(agg)
    for c in halos:
        c.wait()

    def edges(k):
        pick = (iota((N + 2 * H, N), 0) == nbr[k : k + 1, :]).astype(F32).astype(BF)
        hid = silu(dot(table[...], pick) + recv).astype(BF)
        msg = dot(w_msg_t, hid)
        mean = jnp.mean(msg, axis=0, keepdims=True)
        msg = msg - mean
        var = jnp.mean(msg * msg, axis=0, keepdims=True)
        scale = lax.rsqrt(var + 1e-05) * mask[k : k + 1, :].astype(F32)
        agg[...] += msg * scale

    for k in range(DEG // 2):
        edges(k)

    mine.wait()
    pltpu.make_async_copy(
        recv_buf.at[pl.ds(0, DOM - 1)], recv_buf.at[pl.ds(0, DOM - 1)], c_rsem
    ).wait()
    got = recv_buf[...].reshape(2 * DOM, MSG)
    holds = (
        (iota((2 * DOM, SLOTS), 1).astype(F32) == got[:, EH : EH + 1].astype(F32))
        .astype(F32)
        .astype(BF)
    )
    summed = lax.dot_general(
        holds, got[:, 0:EH], (((0,), (0,)), ((), ())), preferred_element_type=F32
    )
    coarse_hid = silu(summed + coarse_bias[...]).astype(BF)
    back_buf[...] = dot(holds, coarse_hid).astype(BF).reshape(DOM, 2, EH)
    mine2 = pltpu.make_async_copy(back_buf.at[me], ret_buf.at[me], own_sem.at[1])
    mine2.start()

    def send_back(k, carry):
        t = lax.rem(me + k, DOM)
        pltpu.make_async_remote_copy(
            src_ref=back_buf.at[t],
            dst_ref=ret_buf.at[me],
            send_sem=r_ssem,
            recv_sem=r_rsem,
            device_id=(g, t),
            device_id_type=MESH,
        ).start()
        return carry

    lax.fori_loop(1, DOM, send_back, 0)

    for k in range(DEG // 2, DEG):
        edges(k)
    loads["w_agg"].wait()
    aggregate = (agg[...].T * gain[...]).astype(BF)
    change = silu(base[...] + dot(aggregate, w_agg[...]))
    base[...] = nodes[...].astype(F32) + change
    loads["w_cout"].wait()

    mine2.wait()
    pltpu.make_async_copy(
        ret_buf.at[pl.ds(0, DOM - 1)], ret_buf.at[pl.ds(0, DOM - 1)], r_rsem
    ).wait()
    coarse_out = dot(ret_buf[...].reshape(2 * DOM, EH), w_cout[...]).astype(BF)
    out[...] = (base[...] + dot(spread, coarse_out)).astype(BF)

    pltpu.make_async_copy(
        send_buf.at[pl.ds(0, DOM - 1)], send_buf.at[pl.ds(0, DOM - 1)], c_ssem
    ).wait()
    pltpu.make_async_copy(
        back_buf.at[pl.ds(0, DOM - 1)], back_buf.at[pl.ds(0, DOM - 1)], r_ssem
    ).wait()


def local(
    nodes,
    w_send,
    w_recv,
    edge_bias,
    w_msg,
    msg_gain,
    w_self,
    w_agg,
    w_coarse_in,
    coarse_bias,
    w_coarse_out,
    halo_send,
    neighbours,
    edge_mask,
    restrict_ids,
    coarse_holder_index,
    coarse_slot,
):
    hbm = pl.BlockSpec(memory_space=pltpu.HBM)
    vmem = pl.BlockSpec(memory_space=pltpu.VMEM)
    dma = pltpu.SemaphoreType.DMA
    return pl.pallas_call(
        kernel,
        out_shape=jax.ShapeDtypeStruct((N, D), BF),
        in_specs=[hbm] * 8 + [vmem] * 9,
        out_specs=vmem,
        scratch_shapes=[
            pltpu.VMEM((N, D), BF),
            pltpu.VMEM((D, EH), BF),
            pltpu.VMEM((D, EH), BF),
            pltpu.VMEM((EH, D), BF),
            pltpu.VMEM((D, D), BF),
            pltpu.VMEM((D, D), BF),
            pltpu.VMEM((D, EH), BF),
            pltpu.VMEM((EH, D), BF),
            pltpu.VMEM((EH, N + 2 * H), BF),
            pltpu.VMEM((2, EH, H), BF),
            pltpu.VMEM((DOM, 2, MSG), BF),
            pltpu.VMEM((DOM, 2, MSG), BF),
            pltpu.VMEM((DOM, 2, EH), BF),
            pltpu.VMEM((DOM, 2, EH), BF),
            pltpu.VMEM((D, N), F32),
            pltpu.VMEM((N, D), F32),
            dma((8,)),
            dma((2,)),
            dma((2,)),
            dma(()),
            dma(()),
            dma(()),
            dma(()),
            dma((2,)),
        ],
        compiler_params=pltpu.CompilerParams(
            collective_id=0, has_side_effects=True, vmem_limit_bytes=60 * 1024 * 1024
        ),
    )(
        nodes,
        w_send,
        w_recv,
        w_msg,
        w_self,
        w_agg,
        w_coarse_in,
        w_coarse_out,
        edge_bias.reshape(1, EH),
        msg_gain.reshape(1, D),
        coarse_bias.reshape(1, EH),
        halo_send,
        neighbours.T,
        edge_mask.T,
        restrict_ids.reshape(1, N),
        coarse_holder_index.T,
        coarse_slot.T,
    )


def solution(mesh):
    part = P(("grp", "dom"))
    return jax.shard_map(
        local,
        mesh=mesh,
        in_specs=(part,) + (P(),) * 10 + (part,) * 6,
        out_specs=part,
        check_vma=False,
    )
```

time: 115 us -> 40.7 us (0.35); the launches traced: 113 us -> 40.5 us
  starting transfers between devices: 45.8 us -> 0 us
  Pallas kernels: 0 us -> 38.8 us
  local copies, waits for them, and re-layouts: 26.5 us -> 1.67 us
  waiting for transfers between devices: 17.2 us -> 0 us
  matrix products: 13.4 us -> 0 us
  other arithmetic: 9.69 us -> 0 us
    all_to_all x3 -> x0, starting transfers between devices: 44 us -> none  [the longest x1 18.9 us: local(): lax.all_to_all(slot_buf, 'dom', split_axis=0, concat_axis=0, tiled=True)]
    pallas_call x0 -> x1, Pallas kernels: none -> 38.8 us  [local(): pl.pallas_call(kernel, out_shape=jax.ShapeDtypeStruct((N, D), BF), in_spe...]
    all_to_all x3 -> x0, waiting for transfers between devices: 17.2 us -> none  [the longest x1 12.1 us: local(): lax.all_to_all(back.reshape(group_partners, slot_limit, width), 'dom', sp...]
    gather x9 -> x0, local copies, waits for them, and re-layouts: 14.7 us -> none  [the longest x8 12.5 us: local(): pre = table[neighbours[:, slot]].astype(jnp.float32) + recv_part + edge_bias]
    dot_general x20 -> x0, matrix products: 13.4 us -> none  [the longest x8 4.39 us: local(): message = jnp.dot(hidden, w_msg, preferred_element_type=jnp.float32)]
    unnamed x122 -> x1, local copies, waits for them, and re-layouts: 7.57 us -> 1.67 us
    reduce_sum x10 -> x0, other arithmetic: 4.53 us -> none  [the longest x8 4.26 us: local(): var = jnp.mean((message - mean) ** 2, axis=1, keepdims=True)]
    reshape x4 -> x0, local copies, waits for them, and re-layouts: 2.83 us -> none  [the longest x1 0.71 us: local(): back.reshape(group_partners, slot_limit, width)]
  transfers between devices with their start and end apart: 5 -> 0, of which waited for: 2 -> 0; matrix products, arithmetic and copies ran while one was open for 27% -> 0% of each run, Pallas kernels for 0% -> 0%
where the time goes in v1:
time: 40.7 us; the launch traced here: 40.5 us
  Pallas kernels  38.8 us (95%)
  local copies, waits for them, and re-layouts  1.67 us (4%)
    pallas_call x1, Pallas kernels, local(): pl.pallas_call(kernel, out_shape=jax.ShapeDtypeStruct((N, D), BF), in_spe...  38.8 us
    unnamed x1, local copies, waits for them, and re-layouts  1.67 us

profile of v1, /device:TPU:6, one launch (start us, length us, event | category | flops | bytes accessed | tf_op | source)
XLA Modules:
  0.0 40.5 jit_solution(9231030090646525797)
XLA Ops:
  0.0 38.8 %shard_map.163 = bf16[256,512]{1,0:T(8,128)(2,1)} custom-call(bf16[256,512]{1,0:T(8,128)(2,1)} %nodes_h.1, bf16[512,256]{1,0:T(8,128)(2,1)} %w_send_h.1, bf16[512,256]{1,0:T(8,128)(2,1)} %w_recv_h.1, bf16[256,512]{1,0:T(8,128)(2,1)} %w_msg_h.1, bf16[512,512]{1,0:T(8,128)(2,1)} %w_self_h.1, bf16[512,512]{1,0:T(8,128)(2,1)} %w_agg_h.1, ...), custom_call_target="tpu_custom_call" | custom-call | tf_op jit(solution)/shard_map/pallas_call | solution.py:282
  38.8 1.7 %copy.19 = bf16[256,512]{1,0:T(8,128)(2,1)} copy(bf16[256,512]{1,0:T(8,128)(2,1)} %shard_map.163) | data formatting | bytes 524288

commit v2 on v1

v2 whole, which is shorter than its diff:
```python
import jax
import jax.numpy as jnp
from jax import lax
from jax.experimental import pallas as pl
from jax.experimental.pallas import tpu as pltpu
from jax.sharding import PartitionSpec as P

MESH = pl.DeviceIdType.MESH
BF = jnp.bfloat16
F32 = jnp.float32
I32 = jnp.int32

GRP = 8
DOM = 64
ZS = 16
YS = 4
N = 256
D = 512
EH = 256
H = 128
DEG = 8
ROWS = 64
RC = 32
RB = 128
SLOTS = 16
PZ = 4
PROC = YS * PZ
OWN = DOM // PROC
CAP = 2 * OWN
NODES_C = OWN * SLOTS


def iota(shape, dim):
    return lax.broadcasted_iota(I32, shape, dim)


def dot(a, b):
    return jnp.dot(a, b, preferred_element_type=F32)


def silu(v):
    return v * (0.5 + 0.5 * jnp.tanh(0.5 * v))


def kernel(*refs):
    ins, (out,), scratch = refs[:17], refs[17:18], refs[18:]
    bufs, rest = scratch[:17], scratch[17:]
    (
        nodes,
        w_cin,
        own,
        slot,
        ids,
        w_send,
        halo_ids,
        w_recv,
        edge_bias,
        w_msg,
        nbr,
        mask,
        w_self,
        gain,
        w_agg,
        coarse_bias,
        w_cout,
    ) = bufs
    (
        table,
        halo_out,
        send_ids,
        recv_ids,
        send_buf,
        recv_buf,
        back_buf,
        ret_buf,
        agg,
        base,
        load_sem,
        halo_ssem,
        halo_rsem,
        i_ssem,
        i_rsem,
        c_ssem,
        c_rsem,
        r_ssem,
        r_rsem,
        own_sem,
    ) = rest
    g = lax.axis_index("grp")
    me = lax.axis_index("dom")
    my_y, my_z = me // ZS, lax.rem(me, ZS)
    lower = lax.rem(g + GRP - 1, GRP)
    upper = lax.rem(g + 1, GRP)
    is_proc = my_z < PZ
    my_proc = jnp.where(is_proc, my_z * YS + my_y, 0)

    def proc_device(j):
        return lax.rem(j, YS) * ZS + j // YS

    loads = [pltpu.make_async_copy(ins[i], bufs[i], load_sem.at[i]) for i in range(17)]
    for i in (2, 3, 4, 0, 1):
        loads[i].start()

    barrier = pltpu.get_barrier_semaphore()
    for t in (lower, upper):
        pl.semaphore_signal(barrier, inc=1, device_id=(t, me), device_id_type=MESH)

    def by_z(k):
        return lax.rem(my_y + k, YS) * ZS + k // YS

    @pl.when(is_proc)
    def _():
        def greet(k, carry):
            t = by_z(k)

            @pl.when(t != me)
            def _():
                pl.semaphore_signal(barrier, inc=1, device_id=(g, t), device_id_type=MESH)

            return carry

        lax.fori_loop(0, DOM, greet, 0)

    for i in range(5, 17):
        loads[i].start()

    for i in (2, 3, 4):
        loads[i].wait()
    own_row = own[...].astype(F32)
    eye = iota((ROWS, ROWS), 0) == iota((ROWS, ROWS), 1)
    own_col = jnp.sum(jnp.where(eye, own_row, 0.0), axis=1, keepdims=True)
    before = (own_col == own_row) & (iota((ROWS, ROWS), 0) < iota((ROWS, ROWS), 1))
    rank = jnp.sum(before.astype(F32), axis=0, keepdims=True).astype(I32)
    pos = own[...] * 2 + rank
    place = (iota((2 * DOM, ROWS), 0) == pos).astype(F32).astype(BF)
    value = (lax.rem(own[...], OWN) * SLOTS + slot[...] + 1).astype(F32)
    at_proc = (iota((PROC, ROWS), 0) == pos // CAP).astype(F32).astype(BF)
    at_lane = jnp.where(iota((128, ROWS), 0) == lax.rem(pos, CAP), value, 0.0).astype(BF)
    coarse_ids = (
        lax.dot_general(at_proc, at_lane, (((1,), (1,)), ((), ())), preferred_element_type=F32)
        - 1.0
    )
    send_ids[...] = coarse_ids.reshape(PROC, 1, 128)
    row_of = ids[...] + (iota((1, N), 1) // RB) * RC
    member = (iota((ROWS, N), 0) == row_of).astype(F32).astype(BF)
    spread = dot(place, member)
    collect = spread.astype(BF)

    pl.semaphore_wait(barrier, jnp.where(is_proc, PROC - 1, PROC) + 2)

    def to_procs(src, dst, ssem, rsem):
        def body(k, carry):
            j = lax.rem(my_z * YS + my_y + k, PROC)
            t = proc_device(j)

            @pl.when(t != me)
            def _():
                pltpu.make_async_remote_copy(
                    src_ref=src.at[j],
                    dst_ref=dst.at[me],
                    send_sem=ssem,
                    recv_sem=rsem,
                    device_id=(g, t),
                    device_id_type=MESH,
                ).start()

            return carry

        lax.fori_loop(0, PROC, body, 0)

    def await_bytes(ref, count, sem):
        part = ref.at[pl.ds(0, count)]
        pltpu.make_async_copy(part, part, sem).wait()

    to_procs(send_ids, recv_ids, i_ssem, i_rsem)
    loads[0].wait()
    restricted = (dot(collect, nodes[...]) * 0.25).astype(BF)
    loads[1].wait()
    coarse_in = dot(restricted, w_cin[...]).astype(BF)
    send_buf[...] = coarse_in.reshape(PROC, CAP, EH)
    to_procs(send_buf, recv_buf, c_ssem, c_rsem)

    loads[5].wait()
    loads[6].wait()
    proj = dot(nodes[...], w_send[...]).T.astype(BF)
    table[:, 0:N] = proj
    halos = []
    for i, t in ((0, lower), (1, upper)):
        pick = (iota((N, H), 0) == halo_ids[0, i : i + 1, :]).astype(F32).astype(BF)
        halo_out[i] = dot(proj, pick).astype(BF)
        c = pltpu.make_async_remote_copy(
            src_ref=halo_out.at[i],
            dst_ref=table.at[:, pl.ds(N + H * (1 - i), H)],
            send_sem=halo_ssem.at[i],
            recv_sem=halo_rsem.at[i],
            device_id=(t, me),
            device_id_type=MESH,
        )
        c.start()
        halos.append(c)

    loads[7].wait()
    loads[8].wait()
    recv = (dot(nodes[...], w_recv[...]) + edge_bias[...]).T
    for i in (9, 10, 11, 12, 13, 14, 15, 16):
        loads[i].wait()
    base[...] = dot(nodes[...], w_self[...])
    w_msg_t = w_msg[...].T
    agg[...] = jnp.zeros_like(agg)
    spread = spread.T.astype(BF)
    for c in halos:
        c.wait()

    for k in range(DEG):
        pick = (iota((N + 2 * H, N), 0) == nbr[k : k + 1, :]).astype(F32).astype(BF)
        hid = silu(dot(table[...], pick) + recv).astype(BF)
        msg = dot(w_msg_t, hid)
        mean = jnp.mean(msg, axis=0, keepdims=True)
        msg = msg - mean
        var = jnp.mean(msg * msg, axis=0, keepdims=True)
        scale = lax.rsqrt(var + 1e-05) * mask[k : k + 1, :].astype(F32)
        agg[...] += msg * scale
    aggregate = (agg[...].T * gain[...]).astype(BF)
    change = silu(base[...] + dot(aggregate, w_agg[...]))
    base[...] = nodes[...].astype(F32) + change

    @pl.when(is_proc)
    def _():
        own_ids = pltpu.make_async_copy(send_ids.at[my_proc], recv_ids.at[me], own_sem.at[0])
        own_rows = pltpu.make_async_copy(send_buf.at[my_proc], recv_buf.at[me], own_sem.at[1])
        own_ids.start()
        own_rows.start()
        own_ids.wait()
        await_bytes(recv_ids, DOM - 1, i_rsem)
        got_ids = recv_ids[...].reshape(DOM, 128).astype(BF)
        total = DOM * CAP
        from_dev = (iota((DOM, total), 0) == iota((DOM, total), 1) // CAP).astype(F32).astype(BF)
        by_lane = lax.dot_general(
            got_ids, from_dev, (((0,), (0,)), ((), ())), preferred_element_type=F32
        )[0:CAP]
        mine = iota((CAP, total), 0) == lax.rem(iota((CAP, total), 1), CAP)
        id_row = jnp.sum(jnp.where(mine, by_lane, 0.0), axis=0, keepdims=True)
        holds = (iota((NODES_C, total), 0).astype(F32) == id_row).astype(F32)
        holds_t = holds.T.astype(BF)
        holds = holds.astype(BF)
        own_rows.wait()
        await_bytes(recv_buf, DOM - 1, c_rsem)
        summed = dot(holds, recv_buf[...].reshape(total, EH))
        coarse_hid = silu(summed + coarse_bias[...]).astype(BF)
        back_buf[...] = dot(holds_t, coarse_hid).astype(BF).reshape(DOM, CAP, EH)

        def send_back(k, carry):
            t = by_z(k)

            @pl.when(t != me)
            def _():
                pltpu.make_async_remote_copy(
                    src_ref=back_buf.at[t],
                    dst_ref=ret_buf.at[my_proc],
                    send_sem=r_ssem,
                    recv_sem=r_rsem,
                    device_id=(g, t),
                    device_id_type=MESH,
                ).start()

            return carry

        lax.fori_loop(0, DOM, send_back, 0)
        own_back = pltpu.make_async_copy(back_buf.at[me], ret_buf.at[my_proc], own_sem.at[2])
        own_back.start()
        own_back.wait()
        await_bytes(send_ids, PROC - 1, i_ssem)
        await_bytes(send_buf, PROC - 1, c_ssem)
        await_bytes(ret_buf, PROC - 1, r_rsem)

    @pl.when(jnp.logical_not(is_proc))
    def _():
        await_bytes(send_ids, PROC, i_ssem)
        await_bytes(send_buf, PROC, c_ssem)
        await_bytes(ret_buf, PROC, r_rsem)

    coarse_out = dot(ret_buf[...].reshape(2 * DOM, EH), w_cout[...]).astype(BF)
    out[...] = (base[...] + dot(spread, coarse_out)).astype(BF)

    @pl.when(is_proc)
    def _():
        await_bytes(back_buf, DOM - 1, r_ssem)


def local(
    nodes,
    w_send,
    w_recv,
    edge_bias,
    w_msg,
    msg_gain,
    w_self,
    w_agg,
    w_coarse_in,
    coarse_bias,
    w_coarse_out,
    halo_send,
    neighbours,
    edge_mask,
    restrict_ids,
    coarse_holder_index,
    coarse_slot,
):
    hbm = pl.BlockSpec(memory_space=pltpu.HBM)
    dma = pltpu.SemaphoreType.DMA
    args = (
        nodes,
        w_coarse_in,
        coarse_holder_index.T,
        coarse_slot.T,
        restrict_ids.reshape(1, N),
        w_send,
        halo_send,
        w_recv,
        edge_bias.reshape(1, EH),
        w_msg,
        neighbours.T,
        edge_mask.T,
        w_self,
        msg_gain.reshape(1, D),
        w_agg,
        coarse_bias.reshape(1, EH),
        w_coarse_out,
    )
    return pl.pallas_call(
        kernel,
        out_shape=jax.ShapeDtypeStruct((N, D), BF),
        in_specs=[hbm] * len(args),
        out_specs=pl.BlockSpec(memory_space=pltpu.VMEM),
        scratch_shapes=[pltpu.VMEM(a.shape, a.dtype) for a in args]
        + [
            pltpu.VMEM((EH, N + 2 * H), BF),
            pltpu.VMEM((2, EH, H), BF),
            pltpu.VMEM((PROC, 1, 128), F32),
            pltpu.VMEM((DOM, 1, 128), F32),
            pltpu.VMEM((PROC, CAP, EH), BF),
            pltpu.VMEM((DOM, CAP, EH), BF),
            pltpu.VMEM((DOM, CAP, EH), BF),
            pltpu.VMEM((PROC, CAP, EH), BF),
            pltpu.VMEM((D, N), F32),
            pltpu.VMEM((N, D), F32),
            dma((len(args),)),
            dma((2,)),
            dma((2,)),
            dma(()),
            dma(()),
            dma(()),
            dma(()),
            dma(()),
            dma(()),
            dma((3,)),
        ],
        compiler_params=pltpu.CompilerParams(
            collective_id=0, has_side_effects=True, vmem_limit_bytes=60 * 1024 * 1024
        ),
    )(*args)


def solution(mesh):
    part = P(("grp", "dom"))
    return jax.shard_map(
        local,
        mesh=mesh,
        in_specs=(part,) + (P(),) * 10 + (part,) * 6,
        out_specs=part,
        check_vma=False,
    )
```

time: 40.7 us -> 36.3 us (0.89)
  the two profiles are of different devices: /device:TPU:6 before, /device:TPU:2 now
where the time goes in v2:
time: 36.3 us; the launch traced here: 36.1 us
  Pallas kernels  34.5 us (95%)
  local copies, waits for them, and re-layouts  1.67 us (5%)
    pallas_call x1, Pallas kernels, local(): pl.pallas_call(kernel, out_shape=jax.ShapeDtypeStruct((N, D), BF), in_spe...  34.5 us
    unnamed x1, local copies, waits for them, and re-layouts  1.67 us

profile of v2, /device:TPU:2, one launch (start us, length us, event | category | flops | bytes accessed | tf_op | source)
XLA Modules:
  0.0 36.1 jit_solution(12227060469643611731)
XLA Ops:
  0.0 34.5 %shard_map.163 = bf16[256,512]{1,0:T(8,128)(2,1)} custom-call(bf16[256,512]{1,0:T(8,128)(2,1)} %refs_0_.1, bf16[512,256]{1,0:T(8,128)(2,1)} %refs_1_.1, s32[1,64]{1,0:T(1,128)} %bitcast.14, s32[1,64]{1,0:T(1,128)} %bitcast.15, s32[1,256]{1,0:T(1,128)} %bitcast.11, bf16[512,256]{1,0:T(8,128)(2,1)} %refs_5_.1, s32[1,2,128]{2,1,0:T(2,128)} %refs_6_.1, ...), custom_call_target="tpu_custom_call" | custom-call | tf_op jit(solution)/shard_map/pallas_call | solution.py:330
  34.5 1.7 %copy.19 = bf16[256,512]{1,0:T(8,128)(2,1)} copy(bf16[256,512]{1,0:T(8,128)(2,1)} %shard_map.163) | data formatting | bytes 524288

commit v3 on v2

--- a/solution.py
+++ b/solution.py
@@ -146,8 +146,6 @@
     spread = dot(place, member)
     collect = spread.astype(BF)
 
-    pl.semaphore_wait(barrier, jnp.where(is_proc, PROC - 1, PROC) + 2)
-
     def to_procs(src, dst, ssem, rsem):
         def body(k, carry):
             j = lax.rem(my_z * YS + my_y + k, PROC)
@@ -172,12 +170,13 @@
         part = ref.at[pl.ds(0, count)]
         pltpu.make_async_copy(part, part, sem).wait()
 
-    to_procs(send_ids, recv_ids, i_ssem, i_rsem)
     loads[0].wait()
     restricted = (dot(collect, nodes[...]) * 0.25).astype(BF)
     loads[1].wait()
     coarse_in = dot(restricted, w_cin[...]).astype(BF)
     send_buf[...] = coarse_in.reshape(PROC, CAP, EH)
+    pl.semaphore_wait(barrier, jnp.where(is_proc, PROC - 1, PROC) + 2)
+    to_procs(send_ids, recv_ids, i_ssem, i_rsem)
     to_procs(send_buf, recv_buf, c_ssem, c_rsem)
 
     loads[5].wait()
@@ -356,9 +355,9 @@
             dma((3,)),
         ],
         compiler_params=pltpu.CompilerParams(
-            collective_id=0, has_side_effects=True, vmem_limit_bytes=60 * 1024 * 1024
+            collective_id=0, has_side_effects=True, vmem_limit_bytes=32 * 1024 * 1024
         ),
-    )(*args)
+    )(*(pltpu.with_memory_space_constraint(a, pltpu.HBM) for a in args))
 
 
 def solution(mesh):

time: 36.3 us -> 32.8 us (0.904)
  the two profiles are of different devices: /device:TPU:2 before, /device:TPU:6 now
where the time goes in v3:
time: 32.8 us; the launch traced here: 32.2 us
  Pallas kernels  31.5 us (96%)
  local copies, waits for them, and re-layouts  0.71 us (2%)
    pallas_call x1, Pallas kernels, local(): pl.pallas_call(kernel, out_shape=jax.ShapeDtypeStruct((N, D), BF), in_spe...  31.5 us
    unnamed x1, local copies, waits for them, and re-layouts  0.71 us

profile of v3, /device:TPU:6, one launch (start us, length us, event | category | flops | bytes accessed | tf_op | source)
XLA Modules:
  0.0 32.2 jit_solution(210308850948941193)
XLA Ops:
  0.0 31.5 %shard_map.163 = bf16[256,512]{1,0:T(8,128)(2,1)S(1)} custom-call(bf16[256,512]{1,0:T(8,128)(2,1)} %refs_0_.1, bf16[512,256]{1,0:T(8,128)(2,1)} %refs_1_.1, s32[1,64]{1,0:T(1,128)} %bitcast.14, s32[1,64]{1,0:T(1,128)} %bitcast.15, s32[1,256]{1,0:T(1,128)} %bitcast.11, bf16[512,256]{1,0:T(8,128)(2,1)} %refs_5_.1, s32[1,2,128]{2,1,0:T(2,128)} %refs_6_.1, ...), custom_call_target="tpu_custom_call" | custom-call | tf_op jit(solution)/shard_map/pallas_call | solution.py:329
  31.5 0.7 %copy.19 = bf16[256,512]{1,0:T(8,128)(2,1)} copy(bf16[256,512]{1,0:T(8,128)(2,1)S(1)} %shard_map.163) | data formatting | bytes 524288

commit v4 on v3

--- a/solution.py
+++ b/solution.py
@@ -148,7 +148,7 @@
 
     def to_procs(src, dst, ssem, rsem):
         def body(k, carry):
-            j = lax.rem(my_z * YS + my_y + k, PROC)
+            j = k // YS * YS + lax.rem(my_y + k, YS)
             t = proc_device(j)
 
             @pl.when(t != me)

time: 32.8 us -> 32.4 us (0.988); the launches traced: 32.2 us -> 32.3 us
  no operation moved by 1% of the time
where the time goes in v4:
time: 32.4 us; the launch traced here: 32.3 us
  Pallas kernels  31.6 us (98%)
  local copies, waits for them, and re-layouts  0.71 us (2%)
    pallas_call x1, Pallas kernels, local(): pl.pallas_call(kernel, out_shape=jax.ShapeDtypeStruct((N, D), BF), in_spe...  31.6 us
    unnamed x1, local copies, waits for them, and re-layouts  0.71 us

profile of v4, /device:TPU:6, one launch (start us, length us, event | category | flops | bytes accessed | tf_op | source)
XLA Modules:
  0.0 32.3 jit_solution(10875578595967993950)
XLA Ops:
  0.0 31.6 %shard_map.163 = bf16[256,512]{1,0:T(8,128)(2,1)S(1)} custom-call(bf16[256,512]{1,0:T(8,128)(2,1)} %refs_0_.1, bf16[512,256]{1,0:T(8,128)(2,1)} %refs_1_.1, s32[1,64]{1,0:T(1,128)} %bitcast.14, s32[1,64]{1,0:T(1,128)} %bitcast.15, s32[1,256]{1,0:T(1,128)} %bitcast.11, bf16[512,256]{1,0:T(8,128)(2,1)} %refs_5_.1, s32[1,2,128]{2,1,0:T(2,128)} %refs_6_.1, ...), custom_call_target="tpu_custom_call" | custom-call | tf_op jit(solution)/shard_map/pallas_call | solution.py:329
  31.6 0.7 %copy.19 = bf16[256,512]{1,0:T(8,128)(2,1)} copy(bf16[256,512]{1,0:T(8,128)(2,1)S(1)} %shard_map.163) | data formatting | bytes 524288
